TPU v7x, 256 devices: a whole 4x4x8 slice. The times are simulated.
256 devices in a mesh: section: 4 (over y), tensor: 16 (over z_lo, x, core), dp: 4 (over z_hi).
Axes of the slice: x: 4, y: 4, z: 8 (z_hi: 4, z_lo: 2; z = z_hi * 2 + z_lo), core: 2. Of those that a mesh axis runs over, the one named last changes fastest.
Arguments:
- grad_out: bfloat16 [4, 4, 256, 6144], P('section', 'dp', 'tensor'), may hold values from -6 to 6
- saved_input: bfloat16 [4, 4, 256, 6144], P('section', 'dp', 'tensor'), may hold values from -6 to 6
- pre_act: bfloat16 [4, 4, 256, 12288], P('section', 'dp', None, 'tensor'), may hold values from -8 to 8
- error: float32 [4, 4, 256, 6144], P('section', 'dp', 'tensor'), may hold values from -3 to 3
- w_up: bfloat16 [4, 6144, 12288], P('section', 'dp', 'tensor'), may hold values from -0.078125 to 0.078125
- w_down: bfloat16 [4, 12288, 6144], P('section', 'tensor', 'dp'), may hold values from -0.0546875 to 0.0546875
- q_init: bfloat16 [4, 6144, 128], P('section'), may hold values from -0.078125 to 0.078125
Outputs:
- grad_up: bfloat16 [4, 6144, 12288], P('section', 'dp', 'tensor')
- grad_down: bfloat16 [4, 12288, 6144], P('section', 'tensor', 'dp')
- new_error: float32 [4, 4, 256, 6144], P('section', 'dp', 'tensor')
- received: bfloat16 [4, 4, 256, 6144], P('section', 'dp', 'tensor')
All inputs are finite; a program needn't handle non-finite values.
Results may differ from a plain program's by a relative error of at most 0.03.
Values may be sent and summed in bfloat16 or wider, within the bound.
A program may use at most 128 MiB of HBM per device.

v0:
```python
import jax
import jax.numpy as jnp
from jax import lax
from jax.sharding import PartitionSpec as P


def shifted(value, axis, by):
    size = lax.axis_size(axis)
    pairs = [(i, i + by) for i in range(size) if 0 <= i + by < size]
    return lax.ppermute(value, axis, pairs)


def gelu_tanh(values):
    return jax.nn.gelu(values, approximate=True)


def shards(grad_out, saved_input, pre_act, error, w_up, w_down, q_init):
    grad_rows = grad_out[0, 0]
    input_rows = saved_input[0, 0]
    replicas = lax.axis_size("dp")
    whole_grad, whole_input = (
        lax.all_gather(grad_rows, "tensor", axis=0, tiled=True),
        lax.all_gather(input_rows, "tensor", axis=0, tiled=True),
    )
    cols_grad, cols_input = (
        lax.all_to_all(whole_grad[None], "dp", split_axis=2, concat_axis=0, tiled=True),
        lax.all_to_all(whole_input[None], "dp", split_axis=2, concat_axis=0, tiled=True),
    )
    group_rows = cols_grad.shape[1]
    width_block = cols_grad.shape[2]
    flat_grad = cols_grad.reshape(replicas * group_rows, width_block)
    flat_input = cols_input.reshape(replicas * group_rows, width_block)
    weight_down = w_down[0]
    weight_up = w_up[0]
    own_pre = pre_act[0, 0]
    pre_all = lax.all_gather(own_pre, "dp", axis=0, tiled=True)
    hidden_all = gelu_tanh(pre_all.astype(jnp.float32)).astype(jnp.bfloat16)
    down_grad = lax.dot_general(
        hidden_all, flat_grad, (((0,), (0,)), ((), ())), preferred_element_type=jnp.float32
    ).astype(jnp.bfloat16)
    grad_hidden = lax.psum_scatter(
        lax.dot_general(
            flat_grad, weight_down, (((1,), (1,)), ((), ())), preferred_element_type=jnp.float32
        ),
        "dp",
        scatter_dimension=0,
        tiled=True,
    )
    grad_pre = jax.vjp(gelu_tanh, own_pre.astype(jnp.float32))[1](grad_hidden)[0].astype(
        jnp.bfloat16
    )
    grad_pre_all = lax.all_gather(grad_pre, "dp", axis=0, tiled=True)
    up_grad = lax.dot_general(
        flat_input, grad_pre_all, (((0,), (0,)), ((), ())), preferred_element_type=jnp.float32
    ).astype(jnp.bfloat16)
    partial_cols = lax.dot_general(
        grad_pre_all, weight_up, (((1,), (1,)), ((), ())), preferred_element_type=jnp.float32
    )
    factor_q = q_init[0].astype(jnp.float32)
    summed_cols = lax.psum_scatter(
        partial_cols.reshape(replicas, group_rows, width_block),
        "tensor",
        scatter_dimension=1,
        tiled=True,
    )
    back_rows = lax.all_to_all(summed_cols, "dp", split_axis=0, concat_axis=2, tiled=True)[0]
    merged = grad_rows.astype(jnp.float32) + back_rows + error[0, 0]
    left = jnp.dot(merged, factor_q, precision=lax.Precision.HIGHEST)
    gram = lax.psum(jnp.dot(left.T, left, precision=lax.Precision.HIGHEST), "tensor")
    lower = jnp.linalg.cholesky(gram)
    factor_left = jax.scipy.linalg.solve_triangular(lower, left.T, lower=True).T.astype(
        jnp.bfloat16
    )
    left_wide = factor_left.astype(jnp.float32)
    right = lax.psum(
        jnp.dot(merged.T, left_wide, precision=lax.Precision.HIGHEST).astype(jnp.bfloat16), "tensor"
    )
    new_error = merged - jnp.dot(factor_left, right.T, preferred_element_type=jnp.float32)
    recv_left, recv_right = shifted((factor_left, right), "section", -1)
    received = jnp.dot(recv_left, recv_right.T, preferred_element_type=jnp.float32).astype(
        jnp.bfloat16
    )
    return (up_grad[None], down_grad[None], new_error[None, None], received[None, None])


def solution(mesh):
    in_specs = (
        P("section", "dp", "tensor", None),
        P("section", "dp", "tensor", None),
        P("section", "dp", None, "tensor"),
        P("section", "dp", "tensor", None),
        P("section", "dp", "tensor"),
        P("section", "tensor", "dp"),
        P("section", None, None),
    )
    out_specs = (
        P("section", "dp", "tensor"),
        P("section", "tensor", "dp"),
        P("section", "dp", "tensor", None),
        P("section", "dp", "tensor", None),
    )
    return jax.shard_map(shards, mesh=mesh, in_specs=in_specs, out_specs=out_specs, check_vma=False)
```

profile of v0, /device:TPU:2, one launch (start us, length us, event | category | flops | bytes accessed | tf_op | source)
XLA Modules:
  0.0 783.5 jit_solution(11111559442568793183)
XLA Ops:
  8.0 42.9 %all-gather.10.cloned.1.call-done = bf16[1,1,256,6144]{3,2,1,0:T(8,128)(2,1)} async-done(((bf16[1,1,16,6144]{3,2,1,0:T(8,128)(2,1)}), bf16[1,1,256,6144]{3,2,1,0:T(8,128)(2,1)}) %all-gather.10.cloned.1.call-update) | async-done | bytes 3145744 | tf_op jit(solution)/shard_map/all_gather | solution.py:22
  50.9 14.0 %copy.28 = bf16[1,256,6144]{1,0,2:T(2,128)(2,1)} copy(bf16[1,256,6144]{2,1,0:T(8,128)(2,1)} %bitcast.102) | data formatting | bytes 6291456 | tf_op jit(solution)/shard_map/broadcast_in_dim | solution.py:26
  65.4 33.2 %reduce.6 = bf16[6144,256]{1,0:T(8,128)(2,1)} reduce(bf16[6144,1,256]{2,1,0:T(2,128)(2,1)} %bitcast.89, bf16[]{:T(256)} %broadcast.74), dimensions={1}, to_apply=%bitcast.72.reduce_sub_computation | reduce | bytes 6291458
  98.6 4.5 reshape.42
  103.1 73.0 %all_to_all.45 = bf16[4,2,196608]{2,1,0:T(2,128)(2,1)} all-to-all(bf16[4,2,196608]{2,1,0:T(2,128)(2,1)} %reshape.42), channel_id=1, replica_groups=mesh['section'=4,'tensor'=16,'dp'=4] {'dp'}, dimensions={0} | all-to-all | bytes 6291456 | tf_op jit(solution)/shard_map/all_to_all | solution.py:26
  176.1 6.2 reshape.43
  182.2 5.0 copy.38
  187.2 4.7 copy.29
  191.9 6.9 fusion.12
  198.9 71.2 %reduce-scatter.3.cloned.1.call-done = f32[256,768]{1,0:T(8,128)} async-done(((f32[1024,768]{1,0:T(8,128)}), f32[256,768]{1,0:T(8,128)}) %reduce-scatter.3.cloned.1.call-update) | async-done | bytes 786448 | tf_op jit(solution)/shard_map/reduce_scatter | solution.py:41
  272.6 41.5 %all-gather.8.cloned.1.call-done = bf16[1024,768]{1,0:T(8,128)(2,1)} async-done(((bf16[256,768]{1,0:T(8,128)(2,1)}), bf16[1024,768]{1,0:T(8,128)(2,1)}) %all-gather.8.cloned.1.call-update) | async-done | bytes 1572880 | tf_op jit(solution)/shard_map/all_gather | solution.py:52
  314.1 6.1 fusion.10
  320.8 66.8 %reduce-scatter.5.cloned.1.call-done = f32[4,16,1536]{2,1,0:T(8,128)} async-done(((f32[4,256,1536]{2,1,0:T(8,128)}), f32[4,16,1536]{2,1,0:T(8,128)}) %reduce-scatter.5.cloned.1.call-update) | async-done | bytes 393232 | tf_op jit(solution)/shard_map/reduce_scatter | solution.py:60
  387.6 18.0 %all_to_all.46 = f32[4,16,1536]{2,1,0:T(8,128)S(1)} all-to-all(f32[4,16,1536]{2,1,0:T(8,128)} %reduce-scatter.5.cloned.1.call-done), channel_id=1, replica_groups=mesh['section'=4,'tensor'=16,'dp'=4] {'dp'}, dimensions={0} | all-to-all | bytes 786432 | tf_op jit(solution)/shard_map/all_to_all | solution.py:66
  407.9 22.6 %all-gather.12.cloned.1.call-done = bf16[1,1,256,6144]{3,2,1,0:T(8,128)(2,1)} async-done(((bf16[1,1,16,6144]{3,2,1,0:T(8,128)(2,1)}), bf16[1,1,256,6144]{3,2,1,0:T(8,128)(2,1)}) %all-gather.12.cloned.1.call-update) | async-done | bytes 3145744 | tf_op jit(solution)/shard_map/all_gather | solution.py:23
  430.5 14.0 %copy.30 = bf16[1,256,6144]{1,0,2:T(2,128)(2,1)} copy(bf16[1,256,6144]{2,1,0:T(8,128)(2,1)} %bitcast.101) | data formatting | bytes 6291456 | tf_op jit(solution)/shard_map/broadcast_in_dim | solution.py:27
  444.5 33.2 %reduce.7 = bf16[6144,256]{1,0:T(8,128)(2,1)} reduce(bf16[6144,1,256]{2,1,0:T(2,128)(2,1)} %bitcast.90, bf16[]{:T(256)} %broadcast.74), dimensions={1}, to_apply=%bitcast.74.reduce_sub_computation | reduce | bytes 6291458
  477.7 4.5 reshape.44
  482.2 5.9 all-to-all-start.1
  488.2 60.2 %all-reduce.3.cloned.1.call-done = f32[128,128]{0,1:T(8,128)} async-done(((f32[128,128]{0,1:T(8,128)}), f32[128,128]{0,1:T(8,128)}) %all-reduce.3.cloned.1.call-update) | async-done | bytes 65552 | tf_op jit(solution)/shard_map/psum | solution.py:69
  550.2 11.7 %cholesky.16 = f32[128,128]{1,0:T(8,128)S(1)} custom-call(f32[128,128]{1,0:T(8,128)S(1)} %fusion.38), custom_call_target="Cholesky" | custom-call | tf_op jit(solution)/shard_map/jit(cholesky)/cholesky | solution.py:70
  563.3 9.8 %custom-call.7 = f32[1,128,128]{1,2,0:T(8,128)S(1)} custom-call(f32[1,128,128]{2,1,0:T(8,128)S(1)} %fusion.36), custom_call_target="InvertDiagBlocksLowerTriangular" | custom-call | tf_op jit(solution)/shard_map/jit(_solve_triangular)/triangular_solve | solution.py:71
  573.3 3.7 convolution_convert_fusion
  577.8 126.1 %all-reduce.5.cloned.1.call-done = bf16[6144,128]{1,0:T(8,128)(2,1)} async-done(((bf16[6144,128]{1,0:T(8,128)(2,1)}), bf16[6144,128]{1,0:T(8,128)(2,1)}) %all-reduce.5.cloned.1.call-update) | async-done | bytes 1572880 | tf_op jit(solution)/shard_map/psum | solution.py:75
  705.4 6.2 reshape.45
  711.6 5.0 copy.39
  716.6 4.6 copy.31
  721.2 32.1 %all-gather.14.cloned.1.call-done = bf16[1,1,1024,768]{3,2,1,0:T(8,128)(2,1)} async-done(((bf16[1,1,256,768]{3,2,1,0:T(8,128)(2,1)}), bf16[1,1,1024,768]{3,2,1,0:T(8,128)(2,1)}) %all-gather.14.cloned.1.call-update) | async-done | bytes 1572880 | tf_op jit(solution)/shard_map/all_gather | solution.py:36
  753.3 6.8 fusion.9
  760.1 4.0 fusion.8
  764.2 4.4 copy.36
  769.9 2.7 fusion
  (51 shorter events, 17.8 us)
Async XLA Ops:
  7.2 306.9 %copy-start = (bf16[1,1536,768]{2,1,0:T(8,128)(2,1)S(1)}, bf16[1,1536,768]{2,1,0:T(8,128)(2,1)}, u32[]{:S(2)}) copy-start(bf16[1,1536,768]{2,1,0:T(8,128)(2,1)} %param.11) | copy-start | bytes 7077892
  7.2 43.7 %all-gather.10.cloned.1.call-start = ((), (), s32[]{:S(2)}) async-start(), calls=%async_computation.10 | async-start | bytes 3342336 | tf_op jit(solution)/shard_map/all_gather | solution.py:22
  7.9 262.2 %reduce-scatter.3.cloned.1.call-start = ((), (), s32[]{:S(2)}) async-start(), calls=%async_computation.5 | async-start | bytes 3932160 | tf_op jit(solution)/shard_map/reduce_scatter | solution.py:41
  198.8 71.3 %copy-start.6 = (bf16[1,1,256,768]{3,2,1,0:T(8,128)(2,1)S(1)}, bf16[1,1,256,768]{3,2,1,0:T(8,128)(2,1)}, u32[]{:S(2)}) copy-start(bf16[1,1,256,768]{3,2,1,0:T(8,128)(2,1)} %param.9) | copy-start | bytes 1179652
  198.8 115.2 %all-gather.8.cloned.1.call-start = ((), (), s32[]{:S(2)}) async-start(), calls=%async_computation.6 | async-start | bytes 1966080 | tf_op jit(solution)/shard_map/all_gather | solution.py:52
  272.6 115.0 %reduce-scatter.5.cloned.1.call-start = ((), (), s32[]{:S(2)}) async-start(), calls=%async_computation.7 | async-start | bytes 6684672 | tf_op jit(solution)/shard_map/reduce_scatter | solution.py:60
  320.2 86.0 %copy-start.2 = (f32[1,1,16,6144]{3,2,1,0:T(8,128)S(1)}, f32[1,1,16,6144]{3,2,1,0:T(8,128)}, u32[]{:S(2)}) copy-start(f32[1,1,16,6144]{3,2,1,0:T(8,128)} %param.10) | copy-start | bytes 1179652
  320.2 86.0 %copy-start.3 = (bf16[1,1,16,6144]{3,2,1,0:T(8,128)(2,1)S(1)}, bf16[1,1,16,6144]{3,2,1,0:T(8,128)(2,1)}, u32[]{:S(2)}) copy-start(bf16[1,1,16,6144]{3,2,1,0:T(8,128)(2,1)} %param.7) | copy-start | bytes 589828
  320.2 86.0 %copy-start.5 = (bf16[1,6144,128]{2,1,0:T(8,128)(2,1)S(1)}, bf16[1,6144,128]{2,1,0:T(8,128)(2,1)}, u32[]{:S(2)}) copy-start(bf16[1,6144,128]{2,1,0:T(8,128)(2,1)} %param.13) | copy-start | bytes 4718596
  320.2 110.3 %all-gather.12.cloned.1.call-start = ((), (), s32[]{:S(2)}) async-start(), calls=%async_computation.11 | async-start | bytes 3342336 | tf_op jit(solution)/shard_map/all_gather | solution.py:23
  320.8 227.7 %all-reduce.3.cloned.1.call-start = ((), (), s32[]{:S(2)}) async-start(), calls=%async_computation.8 | async-start | bytes 131072 | tf_op jit(solution)/shard_map/psum | solution.py:69
  482.2 223.3 %all-to-all-start.1 = ((bf16[4,2,196608]{2,1,0:T(2,128)(2,1)}), bf16[4,2,196608]{2,1,0:T(2,128)(2,1)}, u32[]{:S(2)}, u32[]{:S(2)}) async-start(bf16[4,2,196608]{2,1,0:T(2,128)(2,1)} %reshape.44), calls=%async_computation.2 | async-start | bytes 6291456 | tf_op jit(solution)/shard_map/all_to_all | solution.py:27
  488.1 215.8 %all-reduce.5.cloned.1.call-start = ((), (), s32[]{:S(2)}) async-start(), calls=%async_computation.9 | async-start | bytes 3145728 | tf_op jit(solution)/shard_map/psum | solution.py:75
  577.0 176.2 %all-gather.14.cloned.1.call-start = ((), (), s32[]{:S(2)}) async-start(), calls=%async_computation.12 | async-start | bytes 1966080 | tf_op jit(solution)/shard_map/all_gather | solution.py:36
  703.9 70.2 %collective-permute-start.1 = (bf16[6144,128]{1,0:T(8,128)(2,1)}, bf16[6144,128]{1,0:T(8,128)(2,1)}, u32[]{:S(2)}, u32[]{:S(2)}) collective-permute-start(bf16[6144,128]{1,0:T(8,128)(2,1)} %all-reduce.5.cloned.1.call-done), channel_id=1, source_target_pairs={{64,0},{128,64},{192,128},{65,1},{129,65},{193,129},{66,2},{130,66... | collective-permute-start | bytes 4718600 | tf_op jit(solution)/shard_map/ppermute | solution.py:10
  721.2 38.9 %copy-start.7 = (bf16[1024,768]{1,0:T(8,128)(2,1)S(1)}, bf16[1024,768]{1,0:T(8,128)(2,1)}, u32[]{:S(2)}) copy-start(bf16[1024,768]{1,0:T(8,128)(2,1)} %all-gather.8.cloned.1.call-done) | copy-start | bytes 4718596
  753.3 6.9 copy-start.4
  764.2 12.5 %copy-start.1 = (bf16[1,1536,768]{2,1,0:T(8,128)(2,1)S(1)}, bf16[1,1536,768]{2,1,0:T(8,128)(2,1)}, u32[]{:S(2)}) copy-start(bf16[1,1536,768]{2,1,0:T(8,128)(2,1)} %param.11) | copy-start | bytes 7077892
  768.6 5.5 collective-permute-start
Sparse Core Ops, SparseCore 0:
  9.9 40.9 all-gather.9
  199.0 71.1 reduce-scatter.2
  272.7 41.3 all-gather.7
  320.3 67.2 reduce-scatter.4
  389.3 41.1 all-gather.11
  433.5 114.8 all-reduce.2
  577.2 126.6 all-reduce.4
  705.7 47.5 all-gather.13
where the time goes:
time: 785 us; the launch traced here: 784 us
  waiting for transfers between devices  467 us (59%)
  other arithmetic  92.6 us (12%)
  blocking collectives  91 us (12%)
  local copies, waits for them, and re-layouts  75.1 us (10%)
  matrix products  34.7 us (4%)
  between operations  14.2 us (2%)
  starting transfers between devices  9.02 us (1%)
    psum x1, waiting for transfers between devices, shards(): lax.psum(jnp.dot(merged.T, left_wide, precision=lax.Precision.HIGHEST).as...  126 us
    all_to_all x1, blocking collectives, shards(): lax.all_to_all(whole_grad[None], 'dp', split_axis=2, concat_axis=0, tiled...  73 us
    reduce_scatter x1, waiting for transfers between devices, shards(): lax.psum_scatter(lax.dot_general(flat_grad, weight_down, (((1,), (1,)), (...  71.2 us
    reduce_scatter x1, waiting for transfers between devices, shards(): lax.psum_scatter(partial_cols.reshape(replicas, group_rows, width_block),...  66.8 us
    unnamed x2, other arithmetic  66.4 us
    psum x1, waiting for transfers between devices, shards(): lax.psum(jnp.dot(left.T, left, precision=lax.Precision.HIGHEST), 'tensor')  60.2 us
    all_gather x1, waiting for transfers between devices, shards(): lax.all_gather(grad_rows, 'tensor', axis=0, tiled=True)  42.9 us
    all_gather x1, waiting for transfers between devices, shards(): grad_pre_all = lax.all_gather(grad_pre, 'dp', axis=0, tiled=True)  41.5 us
  transfers between devices with their start and end apart: 11, of which 9 were waited for; matrix products, arithmetic and copies ran while one was open for 15% of the time, Pallas kernels for 0%

commit v1 on v0

v1 whole, which is shorter than its diff:
```python
import jax
import jax.numpy as jnp
from jax import lax
from jax.experimental import pallas as pl
from jax.experimental.pallas import tpu as pltpu
from jax.sharding import PartitionSpec as P

BF, F32 = jnp.bfloat16, jnp.float32
MESH = pl.DeviceIdType.MESH
ROWS = 16
GROUP = 256
WIDTH = 1536
HIDDEN = 768
MODEL = 6144
RANK = 128
PIECE = 384
K0 = 0.7978845608
K1 = 0.044715
HIGH = lax.Precision.HIGHEST


class Copies:
    def __init__(self, send, recv):
        self.send, self.recv, self.count, self.made = send, recv, 0, []

    def new(self, src, dst, device):
        at = self.count
        self.count += 1
        copy = pltpu.make_async_remote_copy(
            src_ref=src,
            dst_ref=dst,
            send_sem=self.send.at[at],
            recv_sem=self.recv.at[at],
            device_id=device,
            device_id_type=MESH,
        )
        self.made.append(copy)
        return copy

    def start(self, src, dst, device):
        copy = self.new(src, dst, device)
        copy.start()
        return copy

    def finish(self, skip):
        for copy in self.made:
            if not any(copy is other for other in skip):
                copy.wait_send()


def add_slabs(dst, src, count):
    def body(j, _):
        dst[j] = (dst[j].astype(F32) + src[j].astype(F32)).astype(BF)
        return 0

    lax.fori_loop(0, count, body, 0)


def gelu_value(v):
    return 0.5 * v * (1.0 + jnp.tanh(K0 * (v + K1 * (v * v * v))))


def gelu_slope(v):
    square = v * v
    th = jnp.tanh(K0 * (v + K1 * (square * v)))
    return 0.5 * (1.0 + th) + (0.5 * K0) * v * (1.0 - th * th) * (1.0 + (3.0 * K1) * square)


def block_kernel(
    grad, inp, pre, error, w_down, w_up,
    gdown_out, gup_out, merged_out,
    G, X, PRE, GP, WD, WU, H, HF, RSA, RSB, C, SB, X1, X2, Z, D, BK, GD, GU, OWN, ERR, MRG,
    send, recv, local,
):
    t = lax.axis_index("tensor")
    d = lax.axis_index("dp")
    zl, x, c = t // 8, (t // 2) % 4, t % 2
    xr, xl, xo = (x + 1) % 4, (x + 3) % 4, (x + 2) % 4
    dr, dl, do = (d + 1) % 4, (d + 3) % 4, (d + 2) % 4
    sib = {"tensor": zl * 8 + x * 2 + (1 - c)}
    zpeer = {"tensor": (1 - zl) * 8 + x * 2 + c}
    right = {"tensor": zl * 8 + xr * 2 + c}
    left = {"tensor": zl * 8 + xl * 2 + c}
    dpr, dpl, dpo = {"dp": dr}, {"dp": dl}, {"dp": do}
    net = Copies(send, recv)

    loads = {}

    def load(name, at, src, dst):
        copy = pltpu.make_async_copy(src, dst, local.at[at])
        copy.start()
        loads[name] = copy

    def cols(block):
        return pl.ds(pl.multiple_of(block * WIDTH, 128), WIDTH)

    load("G", 0, grad.at[:, cols(d)], G.at[d, zl, x, c])
    load("X", 1, inp.at[:, cols(d)], X.at[d, zl, x, c])
    load("WD", 2, w_down, WD)
    load("PRE", 3, pre, PRE.at[d])
    load("WU", 4, w_up, WU)
    load("OWN", 5, grad, OWN)
    load("ERR", 6, error, ERR)

    barrier = pltpu.get_barrier_semaphore()
    for device in (sib, zpeer, right, left, dpr, dpl, dpo):
        pl.semaphore_signal(barrier, inc=1, device_id=device, device_id_type=MESH)
    pl.semaphore_wait(barrier, 7)

    def scatter(src, dst):
        return [
            net.start(src.at[:, cols(to)], dst.at[d, zl, x, c], {"dp": to}) for to in (dr, dl, do)
        ]

    order = (do, dr, dl, d)

    def gather_first(buf, r):
        own = buf.at[r, zl, x, c]
        return dict(
            z=net.start(own, own, zpeer),
            r=[net.start(own, own, right)],
            l=[net.start(own, own, left)],
            s=[],
        )

    def gather_second(buf, r, state):
        state["z"].wait_recv()
        other = buf.at[r, 1 - zl, x, c]
        state["r"].append(net.start(other, other, right))
        state["l"].append(net.start(other, other, left))
        pair = buf.at[r, :, x, c]
        state["s"].append(net.start(pair, pair, sib))

    def gather_third(buf, r, state):
        for copy in state["r"]:
            copy.wait_recv()
        part = buf.at[r, 0, xl, c]
        state["fr"] = net.start(part, part, right)
        for copy in state["l"]:
            copy.wait_recv()
        part = buf.at[r, 1, xr, c]
        state["fl"] = net.start(part, part, left)
        for at in (xl, xr):
            pair = buf.at[r, :, at, c]
            state["s"].append(net.start(pair, pair, sib))

    def gather_fourth(buf, r, state):
        state["fr"].wait_recv()
        state["fl"].wait_recv()
        pair = buf.at[r, :, xo, c]
        state["s"].append(net.start(pair, pair, sib))

    def gather_last(state):
        for copy in state["s"]:
            copy.wait_recv()

    first = scatter(grad, G)
    loads["G"].wait()
    for copy in first:
        copy.wait_recv()
    g_states = [gather_first(G, r) for r in order]
    for r, state in zip(order, g_states):
        gather_second(G, r, state)
    x_first = scatter(inp, X)
    pre_r = net.start(pre, PRE.at[d], dpr)
    pre_l = net.start(pre, PRE.at[d], dpl)

    def hidden_part(r, store):
        def body(j, _):
            at = pl.ds(pl.multiple_of(j * 256, 256), 256)
            rows = G[r].reshape(GROUP, WIDTH)
            store(
                at,
                lax.dot_general(
                    rows, WD[at, :], (((1,), (1,)), ((), ())), preferred_element_type=F32
                ),
            )
            return 0

        lax.fori_loop(0, HIDDEN // 256, body, 0)

    def store_bf(k):
        def store(at, value):
            H[k, :, at] = value.astype(BF)

        return store

    def store_own(at, value):
        HF[:, at] = value

    top, low = pl.ds(0, 128), pl.ds(128, 128)
    rsa, rsb = [], {}
    gather_third(G, order[0], g_states[0])
    for k, r in enumerate(order):
        if k + 1 < 4:
            gather_third(G, order[k + 1], g_states[k + 1])
        gather_fourth(G, r, g_states[k])
        if k == 0:
            loads["WD"].wait()
        gather_last(g_states[k])
        hidden_part(r, store_own if k == 3 else store_bf(k))
        if k == 0:
            rsa.append(net.start(H.at[0, top], RSA.at[0], dpr))
            rsa.append(net.start(H.at[0, low], RSA.at[1], dpl))
        if k == 1:
            rsb["r_low"] = net.start(H.at[1, low], RSB.at[0, low], dpr)
        if k == 2:
            rsb["l_top"] = net.start(H.at[2, top], RSB.at[1, top], dpl)

    def add_rows(k, base, part):
        def body(j, _):
            at = pl.ds(pl.multiple_of(base + j * 16, 16), 16)
            at_part = pl.ds(pl.multiple_of(j * 16, 16), 16)
            H[k, at, :] = (H[k, at, :].astype(F32) + RSA[part, at_part, :].astype(F32)).astype(BF)
            return 0

        lax.fori_loop(0, 8, body, 0)

    rsa[0].wait_recv()
    add_rows(1, 0, 0)
    rsb["r_top"] = net.start(H.at[1, top], RSB.at[0, top], dpr)
    rsa[1].wait_recv()
    add_rows(2, 128, 1)
    rsb["l_low"] = net.start(H.at[2, low], RSB.at[1, low], dpl)

    loads["X"].wait()
    for copy in x_first:
        copy.wait_recv()
    x_states = [gather_first(X, r) for r in order]

    def own_slope(base):
        def body(j, _):
            at = pl.ds(pl.multiple_of(base + j * 16, 16), 16)
            total = HF[at, :] + RSB[0, at, :].astype(F32) + RSB[1, at, :].astype(F32)
            GP[d, at, :] = (total * gelu_slope(PRE[d, at, :].astype(F32))).astype(BF)
            return 0

        lax.fori_loop(0, 8, body, 0)

    loads["PRE"].wait()
    gp = {}
    for name, half, base in (("top", top, 0), ("low", low, 128)):
        rsb["r_" + name].wait_recv()
        rsb["l_" + name].wait_recv()
        own_slope(base)
        part = GP.at[d, half]
        gp["r_" + name] = net.start(part, part, dpr)
        gp["l_" + name] = net.start(part, part, dpl)

    def up_part(r):
        def body(j, _):
            at = pl.ds(pl.multiple_of(j * 256, 256), 256)
            value = lax.dot_general(
                GP[r], WU[at, :], (((1,), (1,)), ((), ())), preferred_element_type=F32
            )
            C[r, :, :, :, :, at] = value.astype(BF).reshape(2, 4, 2, 16, 256)
            return 0

        lax.fori_loop(0, WIDTH // 256, body, 0)

    def s1(r, st):
        up_part(r)
        st["s"] = net.start(C.at[r, :, :, 1 - c], SB.at[r], sib)

    def s2(r, st):
        st["s"].wait_recv()

        def body(j, _):
            a, b = j // 4, j % 4
            C[r, a, b, c] = (C[r, a, b, c].astype(F32) + SB[r, a, b].astype(F32)).astype(BF)
            return 0

        lax.fori_loop(0, 8, body, 0)
        st["x1r"] = net.start(C.at[r, 0, xo, c], X1.at[r, 0], right)
        st["x1l"] = net.start(C.at[r, 1, xo, c], X1.at[r, 1], left)

    def s3(r, st):
        st["x1r"].wait_recv()
        C[r, 0, xr, c] = (C[r, 0, xr, c].astype(F32) + X1[r, 0].astype(F32)).astype(BF)
        st["x2r"] = net.start(C.at[r, :, xr, c], X2.at[r, 0], right)
        st["x1l"].wait_recv()
        C[r, 1, xl, c] = (C[r, 1, xl, c].astype(F32) + X1[r, 1].astype(F32)).astype(BF)
        st["x2l"] = net.start(C.at[r, :, xl, c], X2.at[r, 1], left)

    def s4(r, st):
        st["x2r"].wait_recv()
        st["x2l"].wait_recv()
        for a in (0, 1):
            C[r, a, x, c] = (
                C[r, a, x, c].astype(F32) + X2[r, 0, a].astype(F32) + X2[r, 1, a].astype(F32)
            ).astype(BF)
        st["z"] = net.start(C.at[r, 1 - zl, x, c], Z.at[r], zpeer)

    def s5(r, st, own=False):
        st["z"].wait_recv()
        D[r] = (C[r, zl, x, c].astype(F32) + Z[r].astype(F32)).astype(BF)
        if not own:
            st["b"] = net.start(D.at[r], BK.at[d], {"dp": r})

    chain = (d, dl, dr, do)
    st = [dict() for _ in chain]
    loads["WU"].wait()
    s1(chain[0], st[0])
    s2(chain[0], st[0])
    s3(chain[0], st[0])

    gp["r_top"].wait_recv()
    part = GP.at[dl, top]
    gp["fr"] = net.start(part, part, dpr)
    gp["l_low"].wait_recv()
    part = GP.at[dr, low]
    gp["fl"] = net.start(part, part, dpl)
    for r, state in zip(order, x_states):
        gather_second(X, r, state)
    gp["r_low"].wait_recv()
    gp["l_top"].wait_recv()
    s1(chain[1], st[1])
    s1(chain[2], st[2])
    s4(chain[0], st[0])
    s2(chain[1], st[1])
    s2(chain[2], st[2])
    s5(chain[0], st[0], own=True)
    s3(chain[1], st[1])
    s3(chain[2], st[2])
    for r, state in zip(order, x_states):
        gather_third(X, r, state)
    pre_r.wait_recv()
    part = PRE.at[dl, top]
    pre_fr = net.start(part, part, dpr)
    pre_l.wait_recv()
    part = PRE.at[dr, low]
    pre_fl = net.start(part, part, dpl)
    s4(chain[1], st[1])
    s4(chain[2], st[2])
    for r, state in zip(order, x_states):
        gather_fourth(X, r, state)
    s5(chain[1], st[1])
    s5(chain[2], st[2])

    def up_grad(lo, hi):
        def body(j, _):
            at = pl.ds(pl.multiple_of(j * 256, 256), 256)
            rows = X[:, :, :, :, :, at].reshape(4 * GROUP, 256)
            value = lax.dot_general(
                rows,
                GP[...].reshape(4 * GROUP, HIDDEN),
                (((0,), (0,)), ((), ())),
                preferred_element_type=F32,
            )
            GU[at, :] = value.astype(BF)
            return 0

        lax.fori_loop(lo, hi, body, 0)

    def activate():
        def body(j, _):
            at = pl.ds(pl.multiple_of((j % 16) * 16, 16), 16)
            PRE[j // 16, at, :] = gelu_value(PRE[j // 16, at, :].astype(F32)).astype(BF)
            return 0

        lax.fori_loop(0, 64, body, 0)

    def down_grad(lo, hi):
        def body(j, _):
            at = pl.ds(pl.multiple_of(j * 256, 256), 256)
            value = lax.dot_general(
                PRE[:, :, at].reshape(4 * GROUP, 256),
                G[...].reshape(4 * GROUP, WIDTH),
                (((0,), (0,)), ((), ())),
                preferred_element_type=F32,
            )
            GD[at, :] = value.astype(BF)
            return 0

        lax.fori_loop(lo, hi, body, 0)

    gp["fr"].wait_recv()
    gp["fl"].wait_recv()
    s1(chain[3], st[3])
    for state in x_states:
        gather_last(state)
    up_grad(0, 2)
    s2(chain[3], st[3])
    up_grad(2, 4)
    s3(chain[3], st[3])
    up_grad(4, 6)
    load("GU", 7, GU, gup_out)
    s4(chain[3], st[3])
    pre_fr.wait_recv()
    pre_fl.wait_recv()
    pre_fr.wait_send()
    pre_fl.wait_send()
    activate()
    s5(chain[3], st[3])
    down_grad(0, 3)
    load("GD", 8, GD, gdown_out)

    for k in (1, 2, 3):
        st[k]["b"].wait_recv()
    loads["OWN"].wait()
    loads["ERR"].wait()
    BK[d] = D[d]
    for b in range(4):
        at = pl.ds(b * WIDTH, WIDTH)
        MRG[:, at] = OWN[:, at].astype(F32) + ERR[:, at] + BK[b].astype(F32)
    load("MRG", 9, MRG, merged_out)
    for name in ("GU", "GD", "MRG"):
        loads[name].wait()
    net.finish(skip=(pre_fr, pre_fl))


def block_call(grad, inp, pre, error, w_down, w_up):
    vm = pltpu.VMEM
    whole = (4, 2, 4, 2, ROWS, WIDTH)
    any_spec = pl.BlockSpec(memory_space=pl.ANY)
    return pl.pallas_call(
        block_kernel,
        out_shape=(
            jax.ShapeDtypeStruct((HIDDEN, WIDTH), BF),
            jax.ShapeDtypeStruct((WIDTH, HIDDEN), BF),
            jax.ShapeDtypeStruct((ROWS, MODEL), F32),
        ),
        in_specs=[any_spec] * 6,
        out_specs=(any_spec,) * 3,
        scratch_shapes=[
            vm(whole, BF),
            vm(whole, BF),
            vm((4, GROUP, HIDDEN), BF),
            vm((4, GROUP, HIDDEN), BF),
            vm((HIDDEN, WIDTH), BF),
            vm((WIDTH, HIDDEN), BF),
            vm((3, GROUP, HIDDEN), BF),
            vm((GROUP, HIDDEN), F32),
            vm((2, 128, HIDDEN), BF),
            vm((2, GROUP, HIDDEN), BF),
            vm(whole, BF),
            vm((4, 2, 4, ROWS, WIDTH), BF),
            vm((4, 2, ROWS, WIDTH), BF),
            vm((4, 2, 2, ROWS, WIDTH), BF),
            vm((4, ROWS, WIDTH), BF),
            vm((4, ROWS, WIDTH), BF),
            vm((4, ROWS, WIDTH), BF),
            vm((HIDDEN, WIDTH), BF),
            vm((WIDTH, HIDDEN), BF),
            vm((ROWS, MODEL), BF),
            vm((ROWS, MODEL), F32),
            vm((ROWS, MODEL), F32),
            pltpu.SemaphoreType.DMA((160,)),
            pltpu.SemaphoreType.DMA((160,)),
            pltpu.SemaphoreType.DMA((10,)),
        ],
        compiler_params=pltpu.CompilerParams(
            collective_id=0, has_side_effects=True, vmem_limit_bytes=56 * 2**20
        ),
        name="block",
    )(grad, inp, pre, error, w_down, w_up)


def factor_inverse(A):
    rows = lax.broadcasted_iota(jnp.int32, (RANK, 1), 0)
    lanes = lax.broadcasted_iota(jnp.int32, (RANK, RANK), 1)

    def body(k, _):
        pivot = A[pl.ds(k, 1), :]
        gram = A[:, pl.ds(0, RANK)]
        column = jnp.sum(jnp.where(lanes == k, gram, 0.0), axis=1, keepdims=True)
        top = jnp.sum(jnp.where(rows == k, column, 0.0), axis=0, keepdims=True)
        inv = lax.rsqrt(top)
        scaled = pivot * inv
        weight = jnp.where(rows > k, column * inv, 0.0)
        A[...] = jnp.where(rows == k, scaled, A[...] - weight * scaled)
        return 0

    lax.fori_loop(0, RANK, body, 0)


def rank_kernel(
    merged, q, err_out, recv_out,
    MB, STACK, MC, LF, A, AP, AR, RR,
    send, recv, local,
):
    s = lax.axis_index("section")
    t = lax.axis_index("tensor")
    above, below = (s + 1) % 4, (s + 3) % 4

    def peer(k):
        return (t + k) % 16

    barrier = pltpu.get_barrier_semaphore()

    def greet(k, _):
        pl.semaphore_signal(
            barrier, inc=1, device_id={"tensor": peer(k)}, device_id_type=MESH
        )
        return 0

    def greet_other(k, _):
        for other in (above, below):
            pl.semaphore_signal(
                barrier,
                inc=1,
                device_id={"section": other, "tensor": peer(k)},
                device_id_type=MESH,
            )
        return 0

    lax.fori_loop(1, 16, greet, 0)
    lax.fori_loop(0, 16, greet_other, 0)
    pl.semaphore_wait(barrier, 47)

    def rc(src, dst, at, device):
        return pltpu.make_async_remote_copy(
            src_ref=src,
            dst_ref=dst,
            send_sem=send.at[at],
            recv_sem=recv.at[at],
            device_id=device,
            device_id_type=MESH,
        )

    def loop(lo, fn):
        def body(k, _):
            fn(k)
            return 0

        lax.fori_loop(lo, 16, body, 0)

    high = merged[...].astype(BF)
    STACK[pl.ds(0, 16), :] = high
    STACK[pl.ds(16, 16), :] = (merged[...] - high.astype(F32)).astype(BF)
    for b in range(16):
        MB[b] = STACK[pl.ds(0, 16), pl.ds(b * PIECE, PIECE)]
    both = jnp.dot(STACK[...], q[...], preferred_element_type=F32)
    LF[t] = both[:16] + both[16:]

    def left_copy(k):
        return rc(LF.at[t], LF.at[t], k, {"tensor": peer(k)})

    def block_copy(k):
        return rc(MB.at[peer(k)], MC.at[t], 16 + k, {"tensor": peer(k)})

    loop(1, lambda k: left_copy(k).start())
    loop(1, lambda k: block_copy(k).start())
    MC[t] = MB[t]
    loop(1, lambda k: left_copy(k).wait_recv())
    all_left = LF[...].reshape(GROUP, RANK)
    A[:, pl.ds(0, RANK)] = lax.dot_general(
        all_left, all_left, (((0,), (0,)), ((), ())), precision=HIGH, preferred_element_type=F32
    )
    A[:, pl.ds(RANK, RANK)] = (
        lax.broadcasted_iota(jnp.int32, (RANK, RANK), 0)
        == lax.broadcasted_iota(jnp.int32, (RANK, RANK), 1)
    ).astype(F32)
    factor_inverse(A)
    ortho = lax.dot_general(
        all_left, A[:, pl.ds(RANK, RANK)], (((1,), (1,)), ((), ())),
        precision=HIGH, preferred_element_type=F32,
    ).astype(BF)
    loop(1, lambda k: block_copy(k).wait_recv())
    right = lax.dot_general(
        MC[...].reshape(GROUP, PIECE), ortho, (((0,), (0,)), ((), ())), preferred_element_type=F32
    ).astype(BF)
    approx = lax.dot_general(
        ortho, right, (((1,), (1,)), ((), ())), preferred_element_type=F32
    ).astype(BF)
    AP[...] = approx.reshape(16, ROWS, PIECE)

    def back_copy(k):
        return rc(AP.at[peer(k)], AR.at[t], 32 + k, {"tensor": peer(k)})

    def relay_copy(k):
        return rc(AP.at[peer(k)], RR.at[t], 48 + k, {"section": below, "tensor": peer(k)})

    loop(1, lambda k: back_copy(k).start())
    loop(0, lambda k: relay_copy(k).start())
    AR[t] = AP[t]
    loop(1, lambda k: back_copy(k).wait_recv())
    for b in range(16):
        at = pl.ds(b * PIECE, PIECE)
        err_out[:, at] = merged[:, at] - AR[b].astype(F32)
    loop(0, lambda k: relay_copy(k).wait_recv())
    for b in range(16):
        at = pl.ds(b * PIECE, PIECE)
        recv_out[:, at] = jnp.where(s == 3, jnp.zeros((ROWS, PIECE), BF), RR[b])
    loop(1, lambda k: left_copy(k).wait_send())
    loop(1, lambda k: block_copy(k).wait_send())
    loop(1, lambda k: back_copy(k).wait_send())
    loop(0, lambda k: relay_copy(k).wait_send())


def rank_call(merged, q):
    vm = pltpu.VMEM
    vm_spec = pl.BlockSpec(memory_space=pltpu.VMEM)
    return pl.pallas_call(
        rank_kernel,
        out_shape=(
            jax.ShapeDtypeStruct((ROWS, MODEL), F32),
            jax.ShapeDtypeStruct((ROWS, MODEL), BF),
        ),
        in_specs=[vm_spec] * 2,
        out_specs=(vm_spec,) * 2,
        scratch_shapes=[
            vm((16, ROWS, PIECE), BF),
            vm((2 * ROWS, MODEL), BF),
            vm((16, ROWS, PIECE), BF),
            vm((16, ROWS, RANK), F32),
            vm((RANK, 2 * RANK), F32),
            vm((16, ROWS, PIECE), BF),
            vm((16, ROWS, PIECE), BF),
            vm((16, ROWS, PIECE), BF),
            pltpu.SemaphoreType.DMA((64,)),
            pltpu.SemaphoreType.DMA((64,)),
            pltpu.SemaphoreType.DMA((2,)),
        ],
        compiler_params=pltpu.CompilerParams(
            collective_id=1, has_side_effects=True, vmem_limit_bytes=32 * 2**20
        ),
        name="rank",
    )(merged, q)


def shards(grad_out, saved_input, pre_act, error, w_up, w_down, q_init):
    grad_down, grad_up, merged = block_call(
        grad_out[0, 0], saved_input[0, 0], pre_act[0, 0], error[0, 0], w_down[0], w_up[0]
    )
    new_error, received = rank_call(merged, q_init[0])
    return (grad_up[None], grad_down[None], new_error[None, None], received[None, None])


def solution(mesh):
    in_specs = (
        P("section", "dp", "tensor", None),
        P("section", "dp", "tensor", None),
        P("section", "dp", None, "tensor"),
        P("section", "dp", "tensor", None),
        P("section", "dp", "tensor"),
        P("section", "tensor", "dp"),
        P("section", None, None),
    )
    out_specs = (
        P("section", "dp", "tensor"),
        P("section", "tensor", "dp"),
        P("section", "dp", "tensor", None),
        P("section", "dp", "tensor", None),
    )
    return jax.shard_map(shards, mesh=mesh, in_specs=in_specs, out_specs=out_specs, check_vma=False)
```

time: 785 us -> 188 us (0.24)
  waiting for transfers between devices: 467 us -> 0 us
  Pallas kernels: 0 us -> 178 us
  other arithmetic: 92.6 us -> 0 us
  blocking collectives: 91 us -> 0 us
  local copies, waits for them, and re-layouts: 75.1 us -> 7.2 us
  matrix products: 34.7 us -> 0 us
  between operations: 14.2 us -> 0.68 us
  starting transfers between devices: 9.02 us -> 0 us
    psum x2 -> x0, waiting for transfers between devices: 186 us -> none  [the longest x1 126 us: shards(): lax.psum(jnp.dot(merged.T, left_wide, precision=lax.Precision.HIGHEST).as...]
    pallas_call x0 -> x2, Pallas kernels: none -> 178 us  [the longest x1 139 us: block_call(): pl.pallas_call(block_kernel, out_shape=(jax.ShapeDtypeStruct((HIDDEN, WID...]
    all_gather x4 -> x0, waiting for transfers between devices: 139 us -> none  [the longest x1 42.9 us: shards(): lax.all_gather(grad_rows, 'tensor', axis=0, tiled=True)]
    reduce_scatter x2 -> x0, waiting for transfers between devices: 138 us -> none  [the longest x1 71.2 us: shards(): lax.psum_scatter(lax.dot_general(flat_grad, weight_down, (((1,), (1,)), (...]
    all_to_all x2 -> x0, blocking collectives: 91 us -> none  [the longest x1 73 us: shards(): lax.all_to_all(whole_grad[None], 'dp', split_axis=2, concat_axis=0, tiled...]
    unnamed x2 -> x0, other arithmetic: 66.4 us -> none
    dot_general x9 -> x0, matrix products: 34.6 us -> none  [the longest x1 6.88 us: shards(): lax.dot_general(flat_grad, weight_down, (((1,), (1,)), ((), ())), preferr...]
    unnamed x25 -> x10, local copies, waits for them, and re-layouts: 36.3 us -> 7.2 us
  transfers between devices with their start and end apart: 11 -> 0, of which waited for: 9 -> 0; matrix products, arithmetic and copies ran while one was open for 15% -> 0% of each run, Pallas kernels for 0% -> 0%
where the time goes in v1:
time: 188 us; the launch traced here: 186 us
  Pallas kernels  178 us (95%)
  local copies, waits for them, and re-layouts  7.2 us (4%)
    pallas_call x1, Pallas kernels, block_call(): pl.pallas_call(block_kernel, out_shape=(jax.ShapeDtypeStruct((HIDDEN, WID...  139 us
    pallas_call x1, Pallas kernels, rank_call(): pl.pallas_call(rank_kernel, out_shape=(jax.ShapeDtypeStruct((ROWS, MODEL)...  38.9 us
    unnamed x10, local copies, waits for them, and re-layouts  7.2 us

profile of v1, /device:TPU:2, one launch (start us, length us, event | category | flops | bytes accessed | tf_op | source)
XLA Modules:
  0.0 185.8 jit_solution(14217125330417772282)
XLA Ops:
  0.6 0.0 copy-start
  0.6 139.0 %block.1 = (bf16[768,1536]{1,0:T(8,128)(2,1)}, bf16[1536,768]{1,0:T(8,128)(2,1)}, f32[16,6144]{1,0:T(8,128)}) custom-call(bf16[16,6144]{1,0:T(8,128)(2,1)} %bitcast.20, bf16[16,6144]{1,0:T(8,128)(2,1)} %bitcast.21, bf16[256,768]{1,0:T(8,128)(2,1)} %bitcast.18, f32[16,6144]{1,0:T(8,128)} %bitcast.19, bf16[768,1536]{1,0:T(8,128)(2,1)} %bitcast.16, ...), custom_call_target="tpu_custom_call" | custom-call | tf_op jit(solution)/shard_map/block/pallas_call | solution.py:416
  139.7 0.0 copy-done
  139.7 0.0 copy-start.1
  139.7 1.0 copy-done.1
  140.7 38.9 %rank.1 = (f32[16,6144]{1,0:T(8,128)S(1)}, bf16[16,6144]{1,0:T(8,128)(2,1)S(1)}) custom-call(f32[16,6144]{1,0:T(8,128)S(1)} %copy-done.1, bf16[6144,128]{1,0:T(8,128)(2,1)S(1)} %bitcast.11), custom_call_target="tpu_custom_call" | custom-call | tf_op jit(solution)/shard_map/rank/pallas_call | solution.py:594
  179.6 0.0 copy-start.2
  179.6 3.4 %copy.15 = bf16[1,1536,768]{2,1,0:T(8,128)(2,1)} copy(bf16[1,1536,768]{2,1,0:T(8,128)(2,1)} %bitcast.15) | data formatting | bytes 4718592
  183.0 0.0 copy-done.2
  183.0 1.4 copy.16
  184.4 0.7 copy.17
  185.2 0.7 copy.18
Async XLA Ops:
  0.6 139.1 %copy-start = (bf16[1,6144,128]{2,1,0:T(8,128)(2,1)S(1)}, bf16[1,6144,128]{2,1,0:T(8,128)(2,1)}, u32[]{:S(2)}) copy-start(bf16[1,6144,128]{2,1,0:T(8,128)(2,1)} %param.13) | copy-start | bytes 4718596
  139.7 1.0 copy-start.1
  179.6 3.4 %copy-start.2 = (bf16[768,1536]{1,0:T(8,128)(2,1)S(1)}, bf16[768,1536]{1,0:T(8,128)(2,1)}, u32[]{:S(2)}) copy-start(bf16[768,1536]{1,0:T(8,128)(2,1)} %get-tuple-element.10) | copy-start | bytes 7077892

commit v2 on v0

v2 whole, which is shorter than its diff:
```python
import jax
import jax.numpy as jnp
from jax import lax
from jax.experimental import pallas as pl
from jax.experimental.pallas import tpu as pltpu
from jax.sharding import PartitionSpec as P

BF, F32 = jnp.bfloat16, jnp.float32
MESH = pl.DeviceIdType.MESH
ROWS = 16
GROUP = 256
WIDTH = 1536
HIDDEN = 768
MODEL = 6144
RANK = 128
PIECE = 384
PARTS = (4, 4, 1, 1)
K0 = 0.7978845608
K1 = 0.044715
HIGH = lax.Precision.HIGHEST


class Tracked:
    def __init__(self, copy):
        self.copy, self.sent, self.received = copy, False, False

    def start(self):
        self.copy.start()

    def wait_send(self):
        self.copy.wait_send()
        self.sent = True

    def wait_recv(self):
        self.copy.wait_recv()
        self.received = True


class Copies:
    def __init__(self, send, recv):
        self.send, self.recv, self.count, self.made = send, recv, 0, []

    def new(self, src, dst, device):
        at = self.count
        self.count += 1
        copy = pltpu.make_async_remote_copy(
            src_ref=src,
            dst_ref=dst,
            send_sem=self.send.at[at],
            recv_sem=self.recv.at[at],
            device_id=device,
            device_id_type=MESH,
        )
        copy = Tracked(copy)
        self.made.append(copy)
        return copy

    def start(self, src, dst, device):
        copy = self.new(src, dst, device)
        copy.start()
        return copy

    def finish(self):
        for copy in self.made:
            if not copy.sent:
                copy.wait_send()


def add_slabs(dst, src, count):
    def body(j, _):
        dst[j] = (dst[j].astype(F32) + src[j].astype(F32)).astype(BF)
        return 0

    lax.fori_loop(0, count, body, 0)


def gelu_value(v):
    return 0.5 * v * (1.0 + jnp.tanh(K0 * (v + K1 * (v * v * v))))


def gelu_slope(v):
    square = v * v
    th = jnp.tanh(K0 * (v + K1 * (square * v)))
    return 0.5 * (1.0 + th) + (0.5 * K0) * v * (1.0 - th * th) * (1.0 + (3.0 * K1) * square)


def factor_inverse(A):
    rows = lax.broadcasted_iota(jnp.int32, (16, RANK), 0)
    lanes = lax.broadcasted_iota(jnp.int32, (16, RANK), 1)
    rows2 = lax.broadcasted_iota(jnp.int32, (16, 2 * RANK), 0)

    def wide(value):
        return jnp.concatenate([value, value], axis=1)

    def body(p, _):
        base = pl.multiple_of(p * 16, 16)
        panel = A[pl.ds(base, 16), :]
        gram = panel[:, :RANK]
        cols = [
            jnp.broadcast_to(
                jnp.sum(jnp.where(lanes == base + j, gram, 0.0), axis=1, keepdims=True), (16, RANK)
            )
            for j in range(16)
        ]
        out = jnp.zeros((16, 2 * RANK), F32)
        for k in range(0, 16, 2):
            one, two = cols[k], cols[k + 1]
            a, b, e = one[k : k + 1], two[k : k + 1], two[k + 1 : k + 2]
            det = a * e - b * b
            inv = 1.0 / det
            below = rows >= k + 2
            m0 = jnp.where(below, (e * one - b * two) * inv, 0.0)
            m1 = jnp.where(below, (a * two - b * one) * inv, 0.0)
            for j in range(k + 2, 16):
                cols[j] = cols[j] - (m0 * cols[j][k : k + 1] + m1 * cols[j][k + 1 : k + 2])
            row0, row1 = panel[k : k + 1], panel[k + 1 : k + 2]
            panel = panel - (wide(m0) * row0 + wide(m1) * row1)
            inv_a = 1.0 / a
            scale0 = lax.rsqrt(a)
            scale1 = lax.rsqrt(det * inv_a)
            new0 = row0 * wide(scale0)
            new1 = (row1 - wide(b * inv_a) * row0) * wide(scale1)
            out = jnp.where(rows2 == k, new0, jnp.where(rows2 == k + 1, new1, out))
        A[pl.ds(base, 16), :] = out
        weights = jnp.where(lanes >= base + 16, out[:, :RANK], 0.0)
        A[...] = A[...] - lax.dot_general(
            weights, out, (((0,), (0,)), ((), ())), precision=HIGH, preferred_element_type=F32
        )
        return 0

    lax.fori_loop(0, RANK // 16, body, 0)


def kernel(
    grad, inp, pre, error, w_down, w_up, q_init,
    gdown_out, gup_out, err_out, recv_out,
    G, X, PRE, GP, WD, WU, H, HF, RSA, RSB, C, SB, X2, BK, GD, GU, OWN, ERR, MRG,
    Q, MB, STACK, MC, LF, A, AP, AR, RR,
    send, recv, send_rank, recv_rank, local,
):
    s = lax.axis_index("section")
    t = lax.axis_index("tensor")
    d = lax.axis_index("dp")
    zl, x, c = t // 8, (t // 2) % 4, t % 2
    xr, xl, xo = (x + 1) % 4, (x + 3) % 4, (x + 2) % 4
    dr, dl, do = (d + 1) % 4, (d + 3) % 4, (d + 2) % 4
    above, below = (s + 1) % 4, (s + 3) % 4
    other_z = (1 - zl) * 8 + x * 2 + c
    sib = {"tensor": zl * 8 + x * 2 + (1 - c)}
    zpeer = {"tensor": other_z}
    right = {"tensor": zl * 8 + xr * 2 + c}
    left = {"tensor": zl * 8 + xl * 2 + c}
    opposite = {"tensor": zl * 8 + xo * 2 + c}
    dpr, dpl = {"dp": dr}, {"dp": dl}
    net = Copies(send, recv)

    def peer(k):
        return (t + k) % 16

    def loop(lo, fn):
        def body(k, _):
            fn(k)
            return 0

        lax.fori_loop(lo, 16, body, 0)

    loads = {}

    def done(name):
        loads[name].wait()


    def load(name, src, dst):
        copy = pltpu.make_async_copy(src, dst, local.at[len(loads)])
        copy.start()
        loads[name] = copy

    def cols(block):
        return pl.ds(pl.multiple_of(block * WIDTH, 128), WIDTH)

    def hail(device):
        pl.semaphore_signal(barrier, inc=1, device_id=device, device_id_type=MESH)

    barrier = pltpu.get_barrier_semaphore()
    for to in (do, dr, dl):
        hail({"dp": to})
        hail({"tensor": other_z, "dp": to})
    loop(1, lambda k: hail({"tensor": peer(k)}))
    loop(0, lambda k: hail({"section": above, "tensor": peer(k)}))
    loop(0, lambda k: hail({"section": below, "tensor": peer(k)}))
    load("G", grad.at[:, cols(d)], G.at[d, zl, x, c])
    load("X", inp.at[:, cols(d)], X.at[d, zl, x, c])
    load("WD", w_down, WD)
    load("PRE", pre, PRE.at[d])
    load("WU", w_up, WU)
    load("OWN", grad, OWN)
    load("ERR", error, ERR)
    load("Q", q_init, Q)
    pl.semaphore_wait(barrier, 53)


    targets = (do, dr, dl, d)

    def scatter(src, dst, k):
        to = targets[k]
        part = dst.at[d, zl, x, c]
        made = [net.start(src.at[:, cols(to)], part, {"tensor": other_z, "dp": to})]
        if k < 3:
            made.append(net.start(src.at[:, cols(to)], part, {"dp": to}))
        return made

    order = (do, dr, dl, d)
    arrive = (0, 2, 1, 3)

    def gather_first(buf, r, copies):
        for copy in copies:
            copy.wait_recv()
        pair = buf.at[r, :, x, c]
        return dict(
            x=[net.start(pair, pair, device) for device in (right, left, opposite)],
            s=[net.start(pair, pair, sib)],
        )

    def gather_second(buf, r, state):
        for copy, at in zip(state["x"], (xl, xr, xo)):
            copy.wait_recv()
            pair = buf.at[r, :, at, c]
            state["s"].append(net.start(pair, pair, sib))

    def gather_last(state):
        for copy in state["s"]:
            copy.wait_recv()

    g_scatter = [scatter(grad, G, 0)]
    done("G")
    g_states = [gather_first(G, order[0], g_scatter[0])]
    g_scatter += [scatter(grad, G, k) for k in (1, 2, 3)]
    for copies in g_scatter:
        for copy in copies:
            copy.wait_send()
    x_scatter = [scatter(inp, X, k) for k in range(4)]

    def hidden_part(r, store):
        store(
            lax.dot_general(
                G[r].reshape(GROUP, WIDTH),
                WD[...],
                (((1,), (1,)), ((), ())),
                preferred_element_type=F32,
            )
        )

    def store_bf(k):
        def store(value):
            H[k] = value.astype(BF)

        return store

    def store_own(value):
        HF[...] = value

    top = [pl.ds(0, 64), pl.ds(64, 64)]
    low = [pl.ds(128, 64), pl.ds(192, 64)]
    rsa, early, late = [], [], []
    for k, r in enumerate(order):
        gather_second(G, r, g_states[k])
        if k == 0:
            for n in (1, 2):
                g_states.append(gather_first(G, order[n], g_scatter[arrive[n]]))
            done("WD")
        if k == 2:
            g_states.append(gather_first(G, order[3], g_scatter[arrive[3]]))
        gather_last(g_states[k])
        hidden_part(r, store_own if k == 3 else store_bf(k))
        if k == 0:
            for q in (0, 1):
                rsa.append(
                    (
                        net.start(H.at[0, top[q]], RSA.at[0, top[q]], dpr),
                        net.start(H.at[0, low[q]], RSA.at[1, top[q]], dpl),
                    )
                )
        if k == 1:
            early_r = net.start(H.at[1, low[0]], RSB.at[0, low[0]], dpr)
        if k == 2:
            early.append((early_r, net.start(H.at[2, top[0]], RSB.at[1, top[0]], dpl)))


    def add_rows(k, base, part, q):
        def body(j, _):
            at = pl.ds(pl.multiple_of(base + q * 64 + j * 16, 16), 16)
            at_part = pl.ds(pl.multiple_of(q * 64 + j * 16, 16), 16)
            H[k, at, :] = (H[k, at, :].astype(F32) + RSA[part, at_part, :].astype(F32)).astype(BF)
            return 0

        lax.fori_loop(0, 4, body, 0)

    done("X")
    x_states = [gather_first(X, order[k], x_scatter[arrive[k]]) for k in range(4)]

    for q in (0, 1):
        rsa[q][0].wait_recv()
        add_rows(1, 0, 0, q)
        late_r = net.start(H.at[1, top[q]], RSB.at[0, top[q]], dpr)
        rsa[q][1].wait_recv()
        add_rows(2, 128, 1, q)
        late.append((late_r, net.start(H.at[2, low[q]], RSB.at[1, low[q]], dpl)))
        if q == 0:
            early.append(
                (
                    net.start(H.at[1, low[1]], RSB.at[0, low[1]], dpr),
                    net.start(H.at[2, top[1]], RSB.at[1, top[1]], dpl),
                )
            )

    def own_slope(half, q):
        def body(j, _):
            at = pl.ds(pl.multiple_of(half * 128 + q * 64 + j * 16, 16), 16)
            to = pl.ds(pl.multiple_of(q * 64 + j * 16, 16), 16)
            total = HF[at, :] + RSB[0, at, :].astype(F32) + RSB[1, at, :].astype(F32)
            GP[d, half, to, :] = (total * gelu_slope(PRE[d, at, :].astype(F32))).astype(BF)
            return 0

        lax.fori_loop(0, 4, body, 0)

    done("PRE")
    gp = []
    for q in (0, 1):
        for copy in early[q] + late[q]:
            copy.wait_recv()
        own_slope(0, q)
        own_slope(1, q)
        part = GP.at[d, :, top[q]]
        gp.append((net.start(part, part, dpr), net.start(part, part, dpl)))

    def pass_on(q):
        gp[q][0].wait_recv()
        part = GP.at[dl, 0, top[q]]
        one = net.start(part, part, dpr)
        gp[q][1].wait_recv()
        part = GP.at[dr, 1, top[q]]
        return one, net.start(part, part, dpl)

    def up_part(r):
        def body(j, _):
            at = pl.ds(pl.multiple_of(j * 768, 256), 768)
            value = lax.dot_general(
                GP[r].reshape(GROUP, HIDDEN),
                WU[at, :],
                (((1,), (1,)), ((), ())),
                preferred_element_type=F32,
            )
            C[r, :, :, :, :, at] = value.astype(BF).reshape(2, 4, 2, 16, 768)
            return 0

        lax.fori_loop(0, WIDTH // 768, body, 0)

    def s1(r, st):
        up_part(r)
        st["s"] = net.start(C.at[r, :, :, 1 - c], SB.at[r], sib)

    def s2(r, st):
        st["s"].wait_recv()

        def add(at):
            def body(a, _):
                C[r, a, at, c] = (
                    C[r, a, at, c].astype(F32) + SB[r, a, at].astype(F32)
                ).astype(BF)
                return 0

            lax.fori_loop(0, 2, body, 0)

        st["x"] = []
        for at, slot, device in ((xo, 2, opposite), (xr, 0, right), (xl, 1, left)):
            add(at)
            st["x"].append(net.start(C.at[r, :, at, c], X2.at[r, slot], device))
        add(x)

    def s4(r, st, own=False):
        for copy in st["x"]:
            copy.wait_recv()
        for a in (0, 1):
            C[r, a, x, c] = (
                (C[r, a, x, c].astype(F32) + X2[r, 0, a].astype(F32))
                + (X2[r, 1, a].astype(F32) + X2[r, 2, a].astype(F32))
            ).astype(BF)
        same, across = C.at[r, zl, x, c], C.at[r, 1 - zl, x, c]
        if own:
            st["b"] = [net.start(across, BK.at[d, zl], zpeer)]
            BK[d, zl] = C[d, zl, x, c]
        else:
            st["b"] = [
                net.start(same, BK.at[d, zl], {"dp": r}),
                net.start(across, BK.at[d, zl], {"tensor": other_z, "dp": r}),
            ]

    chain = (d, dl, dr, do)
    st = [dict() for _ in chain]
    for r, state in zip(order, x_states):
        gather_second(X, r, state)
    done("WU")
    s1(chain[0], st[0])
    fwd = [pass_on(0)]
    s2(chain[0], st[0])
    fwd.append(pass_on(1))
    s1(chain[1], st[1])
    s1(chain[2], st[2])
    s4(chain[0], st[0], own=True)
    s2(chain[1], st[1])
    s2(chain[2], st[2])

    def up_grad(lo, hi):
        def body(j, _):
            at = pl.ds(pl.multiple_of(j * 256, 256), 256)
            rows = X[:, :, :, :, :, at].reshape(4 * GROUP, 256)
            value = lax.dot_general(
                rows,
                GP[...].reshape(4 * GROUP, HIDDEN),
                (((0,), (0,)), ((), ())),
                preferred_element_type=F32,
            )
            GU[at, :] = value.astype(BF)
            return 0

        lax.fori_loop(lo, hi, body, 0)

    def activate(r):
        def body(j, _):
            at = pl.ds(pl.multiple_of(j * 16, 16), 16)
            PRE[r, at, :] = gelu_value(PRE[r, at, :].astype(F32)).astype(BF)
            return 0

        lax.fori_loop(0, 16, body, 0)

    def down_grad(lo, hi):
        def body(j, _):
            at = pl.ds(pl.multiple_of(j * 256, 256), 256)
            value = lax.dot_general(
                PRE[:, :, at].reshape(4 * GROUP, 256),
                G[...].reshape(4 * GROUP, WIDTH),
                (((0,), (0,)), ((), ())),
                preferred_element_type=F32,
            )
            GD[at, :] = value.astype(BF)
            return 0

        lax.fori_loop(lo, hi, body, 0)

    for pair in fwd:
        for copy in pair:
            copy.wait_recv()
    pre_part = [pre.at[pl.ds(0, 128)], pre.at[pl.ds(128, 128)]]
    pre_to = [PRE.at[d, pl.ds(0, 128)], PRE.at[d, pl.ds(128, 128)]]
    pre_a = (net.start(pre_part[0], pre_to[0], dpr), net.start(pre_part[1], pre_to[1], dpl))
    s1(chain[3], st[3])
    s4(chain[1], st[1])
    s4(chain[2], st[2])
    for state in x_states:
        gather_last(state)
    s2(chain[3], st[3])
    pre_b = (net.start(pre_part[1], pre_to[1], dpr), net.start(pre_part[0], pre_to[0], dpl))
    up_grad(0, 6)
    load("GU", GU, gup_out)
    s4(chain[3], st[3])
    pre_a[0].wait_recv()
    part = PRE.at[dl, pl.ds(0, 128)]
    pre_fr = net.start(part, part, dpr)
    pre_a[1].wait_recv()
    part = PRE.at[dr, pl.ds(128, 128)]
    pre_fl = net.start(part, part, dpl)
    activate(d)

    done("OWN")
    done("ERR")
    for k in range(4):
        for copy in st[k]["b"]:
            copy.wait_recv()
    for b in range(4):
        at = pl.ds(b * WIDTH, WIDTH)
        block = BK[b, 0].astype(F32) + BK[b, 1].astype(F32)
        merged = OWN[:, at].astype(F32) + ERR[:, at] + block
        MRG[:, at] = merged
        high = merged.astype(BF)
        STACK[pl.ds(0, 16), at] = high
        STACK[pl.ds(16, 16), at] = (merged - high.astype(F32)).astype(BF)
    done("Q")
    both = jnp.dot(STACK[...], Q[...], preferred_element_type=F32)
    LF[t] = both[:16] + both[16:]

    def rc(src, dst, at, device):
        return pltpu.make_async_remote_copy(
            src_ref=src,
            dst_ref=dst,
            send_sem=send_rank.at[at],
            recv_sem=recv_rank.at[at],
            device_id=device,
            device_id_type=MESH,
        )

    def left_copy(k):
        return rc(LF.at[t], LF.at[t], k, {"tensor": peer(k)})

    def block_copy(k):
        return rc(MB.at[peer(k)], MC.at[t], 16 + k, {"tensor": peer(k)})

    def back_copy(k):
        return rc(AP.at[peer(k)], AR.at[t], 32 + k, {"tensor": peer(k)})

    def relay_copy(k):
        return rc(AP.at[peer(k)], RR.at[t], 48 + k, {"section": below, "tensor": peer(k)})

    loop(1, lambda k: left_copy(k).start())
    for b in range(16):
        MB[b] = STACK[pl.ds(0, 16), pl.ds(b * PIECE, PIECE)]
    loop(1, lambda k: block_copy(k).start())
    MC[t] = MB[t]
    A[:, pl.ds(RANK, RANK)] = (
        lax.broadcasted_iota(jnp.int32, (RANK, RANK), 0)
        == lax.broadcasted_iota(jnp.int32, (RANK, RANK), 1)
    ).astype(F32)
    loop(1, lambda k: left_copy(k).wait_recv())
    all_left = LF[...].reshape(GROUP, RANK)
    A[:, pl.ds(0, RANK)] = lax.dot_general(
        all_left, all_left, (((0,), (0,)), ((), ())), precision=HIGH, preferred_element_type=F32
    )
    factor_inverse(A)
    ortho = lax.dot_general(
        all_left, A[:, pl.ds(RANK, RANK)], (((1,), (1,)), ((), ())),
        precision=HIGH, preferred_element_type=F32,
    ).astype(BF)
    loop(1, lambda k: block_copy(k).wait_recv())
    factor = lax.dot_general(
        MC[...].reshape(GROUP, PIECE), ortho, (((0,), (0,)), ((), ())), preferred_element_type=F32
    ).astype(BF)
    approx = lax.dot_general(
        ortho, factor, (((1,), (1,)), ((), ())), preferred_element_type=F32
    ).astype(BF)
    AP[...] = approx.reshape(16, ROWS, PIECE)
    loop(1, lambda k: back_copy(k).start())
    loop(0, lambda k: relay_copy(k).start())
    AR[t] = AP[t]

    for copy in pre_b + (pre_fr, pre_fl):
        copy.wait_recv()
    pre_fr.wait_send()
    pre_fl.wait_send()
    for r in (dl, dr, do):
        activate(r)
    down_grad(0, 3)
    load("GD", GD, gdown_out)
    loop(1, lambda k: back_copy(k).wait_recv())
    for b in range(16):
        at = pl.ds(b * PIECE, PIECE)
        err_out[:, at] = MRG[:, at] - AR[b].astype(F32)
    loop(0, lambda k: relay_copy(k).wait_recv())
    for b in range(16):
        at = pl.ds(b * PIECE, PIECE)
        recv_out[:, at] = jnp.where(s == 3, jnp.zeros((ROWS, PIECE), BF), RR[b])
    loop(1, lambda k: left_copy(k).wait_send())
    loop(1, lambda k: block_copy(k).wait_send())
    loop(1, lambda k: back_copy(k).wait_send())
    loop(0, lambda k: relay_copy(k).wait_send())
    done("GU")
    done("GD")
    net.finish()


def call(grad, inp, pre, error, w_down, w_up, q):
    vm = pltpu.VMEM
    whole = (4, 2, 4, 2, ROWS, WIDTH)
    any_spec = pl.BlockSpec(memory_space=pl.ANY)
    vm_spec = pl.BlockSpec(memory_space=pltpu.VMEM)
    return pl.pallas_call(
        kernel,
        out_shape=(
            jax.ShapeDtypeStruct((HIDDEN, WIDTH), BF),
            jax.ShapeDtypeStruct((WIDTH, HIDDEN), BF),
            jax.ShapeDtypeStruct((ROWS, MODEL), F32),
            jax.ShapeDtypeStruct((ROWS, MODEL), BF),
        ),
        in_specs=[any_spec] * 7,
        out_specs=(any_spec, any_spec, vm_spec, vm_spec),
        scratch_shapes=[
            vm(whole, BF),
            vm(whole, BF),
            vm((4, GROUP, HIDDEN), BF),
            vm((4, 2, 128, HIDDEN), BF),
            vm((HIDDEN, WIDTH), BF),
            vm((WIDTH, HIDDEN), BF),
            vm((3, GROUP, HIDDEN), BF),
            vm((GROUP, HIDDEN), F32),
            vm((2, 128, HIDDEN), BF),
            vm((2, GROUP, HIDDEN), BF),
            vm(whole, BF),
            vm((4, 2, 4, ROWS, WIDTH), BF),
            vm((4, 3, 2, ROWS, WIDTH), BF),
            vm((4, 2, ROWS, WIDTH), BF),
            vm((HIDDEN, WIDTH), BF),
            vm((WIDTH, HIDDEN), BF),
            vm((ROWS, MODEL), BF),
            vm((ROWS, MODEL), F32),
            vm((ROWS, MODEL), F32),
            vm((MODEL, RANK), BF),
            vm((16, ROWS, PIECE), BF),
            vm((2 * ROWS, MODEL), BF),
            vm((16, ROWS, PIECE), BF),
            vm((16, ROWS, RANK), F32),
            vm((RANK, 2 * RANK), F32),
            vm((16, ROWS, PIECE), BF),
            vm((16, ROWS, PIECE), BF),
            vm((16, ROWS, PIECE), BF),
            pltpu.SemaphoreType.DMA((140,)),
            pltpu.SemaphoreType.DMA((140,)),
            pltpu.SemaphoreType.DMA((64,)),
            pltpu.SemaphoreType.DMA((64,)),
            pltpu.SemaphoreType.DMA((10,)),
        ],
        compiler_params=pltpu.CompilerParams(
            collective_id=0, has_side_effects=True, vmem_limit_bytes=58 * 2**20
        ),
        name="block",
    )(grad, inp, pre, error, w_down, w_up, q)


def copy_kernel(*refs):
    sem = refs[12]
    pieces = []
    for n in range(4):
        src, dst, held = refs[n], refs[4 + n], refs[8 + n]
        step = src.shape[0] // PARTS[n]
        for k in range(PARTS[n]):
            at = pl.ds(k * step, step)
            to = len(pieces)
            load = pltpu.make_async_copy(src.at[at], held.at[at], sem.at[0, to])
            load.start()
            store = pltpu.make_async_copy(held.at[at], dst.at[at], sem.at[1, to])
            pieces.append((load, store))
    for load, store in pieces:
        load.wait()
        store.start()
    for load, store in pieces:
        store.wait()


def copy_call(values):
    any_spec = pl.BlockSpec(memory_space=pl.ANY)
    return pl.pallas_call(
        copy_kernel,
        out_shape=tuple(jax.ShapeDtypeStruct(v.shape, v.dtype) for v in values),
        in_specs=[any_spec] * 4,
        out_specs=(any_spec,) * 4,
        scratch_shapes=[pltpu.VMEM(v.shape, v.dtype) for v in values]
        + [pltpu.SemaphoreType.DMA((2, sum(PARTS)))],
        compiler_params=pltpu.CompilerParams(vmem_limit_bytes=16 * 2**20),
        name="deliver",
    )(*values)


def shards(grad_out, saved_input, pre_act, error, w_up, w_down, q_init):
    grad_down, grad_up, new_error, received = call(
        grad_out[0, 0], saved_input[0, 0], pre_act[0, 0], error[0, 0], w_down[0], w_up[0], q_init[0]
    )
    grad_down, grad_up, new_error, received = copy_call((grad_down, grad_up, new_error, received))
    return (grad_up[None], grad_down[None], new_error[None, None], received[None, None])


def solution(mesh):
    in_specs = (
        P("section", "dp", "tensor", None),
        P("section", "dp", "tensor", None),
        P("section", "dp", None, "tensor"),
        P("section", "dp", "tensor", None),
        P("section", "dp", "tensor"),
        P("section", "tensor", "dp"),
        P("section", None, None),
    )
    out_specs = (
        P("section", "dp", "tensor"),
        P("section", "tensor", "dp"),
        P("section", "dp", "tensor", None),
        P("section", "dp", "tensor", None),
    )
    return jax.shard_map(shards, mesh=mesh, in_specs=in_specs, out_specs=out_specs, check_vma=False)
```

time: 785 us -> 153 us (0.19)
  waiting for transfers between devices: 467 us -> 0 us
  Pallas kernels: 0 us -> 144 us
  other arithmetic: 92.6 us -> 0 us
  blocking collectives: 91 us -> 0 us
  local copies, waits for them, and re-layouts: 75.1 us -> 5.24 us
  matrix products: 34.7 us -> 0 us
  between operations: 14.2 us -> 0.65 us
  starting transfers between devices: 9.02 us -> 0 us
    psum x2 -> x0, waiting for transfers between devices: 186 us -> none  [the longest x1 126 us: shards(): lax.psum(jnp.dot(merged.T, left_wide, precision=lax.Precision.HIGHEST).as...]
    pallas_call x0 -> x2, Pallas kernels: none -> 144 us  [the longest x1 140 us: call(): pl.pallas_call(kernel, out_shape=(jax.ShapeDtypeStruct((HIDDEN, WIDTH), B...]
    all_gather x4 -> x0, waiting for transfers between devices: 139 us -> none  [the longest x1 42.9 us: shards(): lax.all_gather(grad_rows, 'tensor', axis=0, tiled=True)]
    reduce_scatter x2 -> x0, waiting for transfers between devices: 138 us -> none  [the longest x1 71.2 us: shards(): lax.psum_scatter(lax.dot_general(flat_grad, weight_down, (((1,), (1,)), (...]
    all_to_all x2 -> x0, blocking collectives: 91 us -> none  [the longest x1 73 us: shards(): lax.all_to_all(whole_grad[None], 'dp', split_axis=2, concat_axis=0, tiled...]
    unnamed x2 -> x0, other arithmetic: 66.4 us -> none
    dot_general x9 -> x0, matrix products: 34.6 us -> none  [the longest x1 6.88 us: shards(): lax.dot_general(flat_grad, weight_down, (((1,), (1,)), ((), ())), preferr...]
    unnamed x25 -> x8, local copies, waits for them, and re-layouts: 36.3 us -> 5.24 us
  transfers between devices with their start and end apart: 11 -> 0, of which waited for: 9 -> 0; matrix products, arithmetic and copies ran while one was open for 15% -> 0% of each run, Pallas kernels for 0% -> 0%
where the time goes in v2:
time: 153 us; the launch traced here: 150 us
  Pallas kernels  144 us (94%)
  local copies, waits for them, and re-layouts  5.24 us (3%)
    pallas_call x1, Pallas kernels, call(): pl.pallas_call(kernel, out_shape=(jax.ShapeDtypeStruct((HIDDEN, WIDTH), B...  140 us
    unnamed x8, local copies, waits for them, and re-layouts  5.24 us
    pallas_call x1, Pallas kernels, copy_call(): pl.pallas_call(copy_kernel, out_shape=tuple((jax.ShapeDtypeStruct(v.shape...  3.92 us

profile of v2, /device:TPU:2, one launch (start us, length us, event | category | flops | bytes accessed | tf_op | source)
XLA Modules:
  0.0 150.3 jit_solution(18286236216427977293)
XLA Ops:
  0.6 140.5 %block.1 = (bf16[768,1536]{1,0:T(8,128)(2,1)}, bf16[1536,768]{1,0:T(8,128)(2,1)}, f32[16,6144]{1,0:T(8,128)}, bf16[16,6144]{1,0:T(8,128)(2,1)}) custom-call(bf16[16,6144]{1,0:T(8,128)(2,1)} %bitcast.16, bf16[16,6144]{1,0:T(8,128)(2,1)} %bitcast.17, bf16[256,768]{1,0:T(8,128)(2,1)} %bitcast.14, f32[16,6144]{1,0:T(8,128)} %bitcast.15, ...), custom_call_target="tpu_custom_call" | custom-call | tf_op jit(solution)/shard_map/block/pallas_call | solution.py:574
  141.1 0.0 copy-start
  141.1 1.7 %copy-done = bf16[768,1536]{1,0:T(8,128)(2,1)S(1)} copy-done((bf16[768,1536]{1,0:T(8,128)(2,1)S(1)}, bf16[768,1536]{1,0:T(8,128)(2,1)}, u32[]{:S(2)}) %copy-start) | copy-done | bytes 2359320
  142.8 0.0 copy-start.1
  142.8 1.7 %copy-done.1 = bf16[1536,768]{1,0:T(8,128)(2,1)S(1)} copy-done((bf16[1536,768]{1,0:T(8,128)(2,1)S(1)}, bf16[1536,768]{1,0:T(8,128)(2,1)}, u32[]{:S(2)}) %copy-start.1) | copy-done | bytes 2359320
  144.5 0.0 copy-start.2
  144.5 1.0 copy-done.2
  145.5 0.0 copy-start.3
  145.5 0.9 copy-done.3
  146.4 3.9 %deliver.1 = (bf16[768,1536]{1,0:T(8,128)(2,1)}, bf16[1536,768]{1,0:T(8,128)(2,1)}, f32[16,6144]{1,0:T(8,128)}, bf16[16,6144]{1,0:T(8,128)(2,1)}) custom-call(bf16[768,1536]{1,0:T(8,128)(2,1)S(1)} %copy-done, bf16[1536,768]{1,0:T(8,128)(2,1)S(1)} %copy-done.1, f32[16,6144]{1,0:T(8,128)S(1)} %copy-done.2, bf16[16,6144]{1,0:T(8,128)(2,1)S(1)} %copy-done.3), custom_call_target="tpu_custom_call" | custom-call | tf_op jit(solution)/shard_map/deliver/pallas_call | solution.py:648
Async XLA Ops:
  141.1 1.7 %copy-start = (bf16[768,1536]{1,0:T(8,128)(2,1)S(1)}, bf16[768,1536]{1,0:T(8,128)(2,1)}, u32[]{:S(2)}) copy-start(bf16[768,1536]{1,0:T(8,128)(2,1)} %get-tuple-element.12.refs_0_) | copy-start | bytes 7077892
  142.8 1.7 %copy-start.1 = (bf16[1536,768]{1,0:T(8,128)(2,1)S(1)}, bf16[1536,768]{1,0:T(8,128)(2,1)}, u32[]{:S(2)}) copy-start(bf16[1536,768]{1,0:T(8,128)(2,1)} %get-tuple-element.13.refs_1_) | copy-start | bytes 7077892
  144.5 1.0 copy-start.2
  145.5 0.9 copy-start.3

commit v3 on v2

--- a/solution.py
+++ b/solution.py
@@ -134,7 +134,7 @@
 def kernel(
     grad, inp, pre, error, w_down, w_up, q_init,
     gdown_out, gup_out, err_out, recv_out,
-    G, X, PRE, GP, WD, WU, H, HF, RSA, RSB, C, SB, X2, BK, GD, GU, OWN, ERR, MRG,
+    G, X, PRE, HID, GP, WD, WU, H, HF, RSA, RSB, C, SB, X2, BK, GD, ACC, GU, OWN, ERR, MRG,
     Q, MB, STACK, MC, LF, A, AP, AR, RR,
     send, recv, send_rank, recv_rank, local,
 ):
@@ -239,6 +239,15 @@
         for copy in copies:
             copy.wait_send()
     x_scatter = [scatter(inp, X, k) for k in range(4)]
+    pre_part = [pre.at[pl.ds(0, 128)], pre.at[pl.ds(128, 128)]]
+    pre_to = [PRE.at[d, pl.ds(0, 128)], PRE.at[d, pl.ds(128, 128)]]
+
+    def pre_first():
+        return (
+            net.start(pre_part[0], pre_to[0], dpr),
+            net.start(pre_part[1], pre_to[1], dpl),
+        )
+
 
     def hidden_part(r, store):
         store(
@@ -428,47 +437,63 @@
     def activate(r):
         def body(j, _):
             at = pl.ds(pl.multiple_of(j * 16, 16), 16)
-            PRE[r, at, :] = gelu_value(PRE[r, at, :].astype(F32)).astype(BF)
+            HID[r, at, :] = gelu_value(PRE[r, at, :].astype(F32)).astype(BF)
             return 0
 
         lax.fori_loop(0, 16, body, 0)
 
-    def down_grad(lo, hi):
+    def down_part(r, at):
+        return lax.dot_general(
+            HID[r, :, at],
+            G[r].reshape(GROUP, WIDTH),
+            (((0,), (0,)), ((), ())),
+            preferred_element_type=F32,
+        )
+
+    def down_first():
         def body(j, _):
             at = pl.ds(pl.multiple_of(j * 256, 256), 256)
-            value = lax.dot_general(
-                PRE[:, :, at].reshape(4 * GROUP, 256),
-                G[...].reshape(4 * GROUP, WIDTH),
-                (((0,), (0,)), ((), ())),
-                preferred_element_type=F32,
-            )
-            GD[at, :] = value.astype(BF)
+            ACC[at, :] = (down_part(d, at) + down_part(dl, at)) + down_part(dr, at)
             return 0
 
-        lax.fori_loop(lo, hi, body, 0)
+        lax.fori_loop(0, 3, body, 0)
+
+    def down_last():
+        def body(j, _):
+            at = pl.ds(pl.multiple_of(j * 256, 256), 256)
+            GD[at, :] = (ACC[at, :] + down_part(do, at)).astype(BF)
+            return 0
+
+        lax.fori_loop(0, 3, body, 0)
+
+    def pre_second():
+        pre_a[0].wait_recv()
+        part = PRE.at[dl, pl.ds(0, 128)]
+        one = net.start(part, part, dpr)
+        pre_a[1].wait_recv()
+        part = PRE.at[dr, pl.ds(128, 128)]
+        return one, net.start(part, part, dpl)
+
+    def pre_third():
+        return (
+            net.start(pre_part[1], pre_to[1], dpr),
+            net.start(pre_part[0], pre_to[0], dpl),
+        )
 
     for pair in fwd:
         for copy in pair:
             copy.wait_recv()
-    pre_part = [pre.at[pl.ds(0, 128)], pre.at[pl.ds(128, 128)]]
-    pre_to = [PRE.at[d, pl.ds(0, 128)], PRE.at[d, pl.ds(128, 128)]]
-    pre_a = (net.start(pre_part[0], pre_to[0], dpr), net.start(pre_part[1], pre_to[1], dpl))
+    pre_a = pre_first()
+    pre_b = pre_third()
     s1(chain[3], st[3])
     s4(chain[1], st[1])
     s4(chain[2], st[2])
     for state in x_states:
         gather_last(state)
     s2(chain[3], st[3])
-    pre_b = (net.start(pre_part[1], pre_to[1], dpr), net.start(pre_part[0], pre_to[0], dpl))
     up_grad(0, 6)
     load("GU", GU, gup_out)
     s4(chain[3], st[3])
-    pre_a[0].wait_recv()
-    part = PRE.at[dl, pl.ds(0, 128)]
-    pre_fr = net.start(part, part, dpr)
-    pre_a[1].wait_recv()
-    part = PRE.at[dr, pl.ds(128, 128)]
-    pre_fl = net.start(part, part, dpl)
     activate(d)
 
     done("OWN")
@@ -520,6 +545,7 @@
         == lax.broadcasted_iota(jnp.int32, (RANK, RANK), 1)
     ).astype(F32)
     loop(1, lambda k: left_copy(k).wait_recv())
+    pre_f = pre_second()
     all_left = LF[...].reshape(GROUP, RANK)
     A[:, pl.ds(0, RANK)] = lax.dot_general(
         all_left, all_left, (((0,), (0,)), ((), ())), precision=HIGH, preferred_element_type=F32
@@ -541,14 +567,11 @@
     loop(0, lambda k: relay_copy(k).start())
     AR[t] = AP[t]
 
-    for copy in pre_b + (pre_fr, pre_fl):
+    for copy in pre_b:
         copy.wait_recv()
-    pre_fr.wait_send()
-    pre_fl.wait_send()
-    for r in (dl, dr, do):
-        activate(r)
-    down_grad(0, 3)
-    load("GD", GD, gdown_out)
+    activate(dl)
+    activate(dr)
+    down_first()
     loop(1, lambda k: back_copy(k).wait_recv())
     for b in range(16):
         at = pl.ds(b * PIECE, PIECE)
@@ -557,6 +580,11 @@
     for b in range(16):
         at = pl.ds(b * PIECE, PIECE)
         recv_out[:, at] = jnp.where(s == 3, jnp.zeros((ROWS, PIECE), BF), RR[b])
+    for copy in pre_f:
+        copy.wait_recv()
+    activate(do)
+    down_last()
+    load("GD", GD, gdown_out)
     loop(1, lambda k: left_copy(k).wait_send())
     loop(1, lambda k: block_copy(k).wait_send())
     loop(1, lambda k: back_copy(k).wait_send())
@@ -585,6 +613,7 @@
             vm(whole, BF),
             vm(whole, BF),
             vm((4, GROUP, HIDDEN), BF),
+            vm((4, GROUP, HIDDEN), BF),
             vm((4, 2, 128, HIDDEN), BF),
             vm((HIDDEN, WIDTH), BF),
             vm((WIDTH, HIDDEN), BF),
@@ -597,6 +626,7 @@
             vm((4, 3, 2, ROWS, WIDTH), BF),
             vm((4, 2, ROWS, WIDTH), BF),
             vm((HIDDEN, WIDTH), BF),
+            vm((HIDDEN, WIDTH), F32),
             vm((WIDTH, HIDDEN), BF),
             vm((ROWS, MODEL), BF),
             vm((ROWS, MODEL), F32),
@@ -652,7 +682,7 @@
         out_specs=(any_spec,) * 4,
         scratch_shapes=[pltpu.VMEM(v.shape, v.dtype) for v in values]
         + [pltpu.SemaphoreType.DMA((2, sum(PARTS)))],
-        compiler_params=pltpu.CompilerParams(vmem_limit_bytes=16 * 2**20),
+        compiler_params=pltpu.CompilerParams(vmem_limit_bytes=60 * 2**20),
         name="deliver",
     )(*values)
 

time: 153 us -> 148 us (0.967)
  local copies, waits for them, and re-layouts: 5.24 us -> 0 us
    unnamed x8 -> x0, local copies, waits for them, and re-layouts: 5.24 us -> none
where the time goes in v3:
time: 148 us; the launch traced here: 145 us
  Pallas kernels  144 us (97%)
    pallas_call x1, Pallas kernels, call(): pl.pallas_call(kernel, out_shape=(jax.ShapeDtypeStruct((HIDDEN, WIDTH), B...  140 us
    pallas_call x1, Pallas kernels, copy_call(): pl.pallas_call(copy_kernel, out_shape=tuple((jax.ShapeDtypeStruct(v.shape...  4.6 us

profile of v3, /device:TPU:2, one launch (start us, length us, event | category | flops | bytes accessed | tf_op | source)
XLA Modules:
  0.0 145.0 jit_solution(13058971688861889473)
XLA Ops:
  0.6 139.8 %block.1 = (bf16[768,1536]{1,0:T(8,128)(2,1)}, bf16[1536,768]{1,0:T(8,128)(2,1)}, f32[16,6144]{1,0:T(8,128)}, bf16[16,6144]{1,0:T(8,128)(2,1)}) custom-call(bf16[16,6144]{1,0:T(8,128)(2,1)} %bitcast.16, bf16[16,6144]{1,0:T(8,128)(2,1)} %bitcast.17, bf16[256,768]{1,0:T(8,128)(2,1)} %bitcast.14, f32[16,6144]{1,0:T(8,128)} %bitcast.15, ...), custom_call_target="tpu_custom_call" | custom-call | tf_op jit(solution)/shard_map/block/pallas_call | solution.py:602
  140.4 4.6 %deliver.1 = (bf16[768,1536]{1,0:T(8,128)(2,1)}, bf16[1536,768]{1,0:T(8,128)(2,1)}, f32[16,6144]{1,0:T(8,128)}, bf16[16,6144]{1,0:T(8,128)(2,1)}) custom-call(bf16[768,1536]{1,0:T(8,128)(2,1)} %get-tuple-element.12.refs_0_, bf16[1536,768]{1,0:T(8,128)(2,1)} %get-tuple-element.13.refs_1_, f32[16,6144]{1,0:T(8,128)} %get-tuple-element.14.refs_2_, ...), custom_call_target="tpu_custom_call" | custom-call | tf_op jit(solution)/shard_map/deliver/pallas_call | solution.py:678

commit v4 on v3

--- a/solution.py
+++ b/solution.py
@@ -415,9 +415,9 @@
     fwd.append(pass_on(1))
     s1(chain[1], st[1])
     s1(chain[2], st[2])
-    s4(chain[0], st[0], own=True)
     s2(chain[1], st[1])
     s2(chain[2], st[2])
+    s4(chain[0], st[0], own=True)
 
     def up_grad(lo, hi):
         def body(j, _):
@@ -459,12 +459,10 @@
         lax.fori_loop(0, 3, body, 0)
 
     def down_last():
-        def body(j, _):
-            at = pl.ds(pl.multiple_of(j * 256, 256), 256)
+        for j in range(3):
+            at = pl.ds(j * 256, 256)
             GD[at, :] = (ACC[at, :] + down_part(do, at)).astype(BF)
-            return 0
-
-        lax.fori_loop(0, 3, body, 0)
+            load(f"GD{j}", GD.at[at], gdown_out.at[at])
 
     def pre_second():
         pre_a[0].wait_recv()
@@ -486,11 +484,11 @@
     pre_a = pre_first()
     pre_b = pre_third()
     s1(chain[3], st[3])
-    s4(chain[1], st[1])
-    s4(chain[2], st[2])
     for state in x_states:
         gather_last(state)
     s2(chain[3], st[3])
+    s4(chain[1], st[1])
+    s4(chain[2], st[2])
     up_grad(0, 6)
     load("GU", GU, gup_out)
     s4(chain[3], st[3])
@@ -584,13 +582,13 @@
         copy.wait_recv()
     activate(do)
     down_last()
-    load("GD", GD, gdown_out)
     loop(1, lambda k: left_copy(k).wait_send())
     loop(1, lambda k: block_copy(k).wait_send())
     loop(1, lambda k: back_copy(k).wait_send())
     loop(0, lambda k: relay_copy(k).wait_send())
     done("GU")
-    done("GD")
+    for j in range(3):
+        done(f"GD{j}")
     net.finish()
 
 
@@ -644,7 +642,7 @@
             pltpu.SemaphoreType.DMA((140,)),
             pltpu.SemaphoreType.DMA((64,)),
             pltpu.SemaphoreType.DMA((64,)),
-            pltpu.SemaphoreType.DMA((10,)),
+            pltpu.SemaphoreType.DMA((12,)),
         ],
         compiler_params=pltpu.CompilerParams(
             collective_id=0, has_side_effects=True, vmem_limit_bytes=58 * 2**20

time: 148 us -> 147 us (level)
  no operation moved by 1% of the time
where the time goes in v4:
time: 147 us; the launch traced here: 144 us
  Pallas kernels  143 us (97%)
    pallas_call x1, Pallas kernels, call(): pl.pallas_call(kernel, out_shape=(jax.ShapeDtypeStruct((HIDDEN, WIDTH), B...  139 us
    pallas_call x1, Pallas kernels, copy_call(): pl.pallas_call(copy_kernel, out_shape=tuple((jax.ShapeDtypeStruct(v.shape...  4.6 us

profile of v4, /device:TPU:2, one launch (start us, length us, event | category | flops | bytes accessed | tf_op | source)
XLA Modules:
  0.0 144.1 jit_solution(18252015879731924723)
XLA Ops:
  0.6 138.9 %block.1 = (bf16[768,1536]{1,0:T(8,128)(2,1)}, bf16[1536,768]{1,0:T(8,128)(2,1)}, f32[16,6144]{1,0:T(8,128)}, bf16[16,6144]{1,0:T(8,128)(2,1)}) custom-call(bf16[16,6144]{1,0:T(8,128)(2,1)} %bitcast.16, bf16[16,6144]{1,0:T(8,128)(2,1)} %bitcast.17, bf16[256,768]{1,0:T(8,128)(2,1)} %bitcast.14, f32[16,6144]{1,0:T(8,128)} %bitcast.15, ...), custom_call_target="tpu_custom_call" | custom-call | tf_op jit(solution)/shard_map/block/pallas_call | solution.py:600
  139.5 4.6 %deliver.1 = (bf16[768,1536]{1,0:T(8,128)(2,1)}, bf16[1536,768]{1,0:T(8,128)(2,1)}, f32[16,6144]{1,0:T(8,128)}, bf16[16,6144]{1,0:T(8,128)(2,1)}) custom-call(bf16[768,1536]{1,0:T(8,128)(2,1)} %get-tuple-element.12.refs_0_, bf16[1536,768]{1,0:T(8,128)(2,1)} %get-tuple-element.13.refs_1_, f32[16,6144]{1,0:T(8,128)} %get-tuple-element.14.refs_2_, ...), custom_call_target="tpu_custom_call" | custom-call | tf_op jit(solution)/shard_map/deliver/pallas_call | solution.py:676
